TPU v7x, 32 devices: a whole 2x2x4 slice. The times are simulated.
32 devices in a mesh: rep: 8 (over y, x, core), et: 4 (over z).
Axes of the slice: x: 2, y: 2, z: 4, core: 2. Of those that a mesh axis runs over, the one named last changes fastest.
Arguments:
- tokens: bfloat16 [4096, 2048], P(('rep', 'et')), parts along dimension 0, may hold values from -6 to 6
- expert_ids: int32 [4096, 2], P(('rep', 'et')), parts along dimension 0, may hold values from 0 to 7, as said below
- route_logits: float32 [4096, 2], P(('rep', 'et')), parts along dimension 0, may hold values from -3 to 3
- w_gate: bfloat16 [2, 7168, 2048], P(None, 'et'), may hold values from -0.125 to 0.125
- w_up: bfloat16 [2, 7168, 2048], P(None, 'et'), may hold values from -0.125 to 0.125
- w_down: bfloat16 [2, 7168, 2048], P(None, 'et'), may hold values from -0.0625 to 0.0625
Outputs:
- mixed: bfloat16 [4096, 2048], P(('rep', 'et')), parts along dimension 0
There are 8 independent parts, one for each index of `rep`. A program takes and returns all parts, laid end to end along the dimension named above; an argument that names none is the same for every part. Nothing has to cross between parts.
Inputs may be any that keep to these rules, and one draw needn't show every extreme that they name: `expert_ids`: each row names two different experts. Within each aligned block of 128 rows (the rows of one device), no expert is named by more than 48 rows, and experts 0 and 1 are each named by exactly 48 rows.
All inputs are finite; a program needn't handle non-finite values.
Results may differ from a plain program's by a relative error of at most 0.015.
Values may be sent and summed in bfloat16 or wider, within the bound.
A program may use at most 128 MiB of HBM per device.

v0:
```python
import jax
import jax.numpy as jnp
from jax import lax
from jax.sharding import PartitionSpec as P

EXP_WIN = 2
CAP = 48


def slot_onehot(routed, capacity):
    ranking = jnp.cumsum(routed.astype(jnp.int32), axis=0) - 1
    slot_of = jnp.where(routed, ranking, capacity)
    numbers = jnp.arange(capacity, dtype=jnp.int32)
    return (slot_of.T[:, None, :] == numbers[None, :, None]).astype(jnp.bfloat16)


def experts_apply(token_rows, weights, w_gate, w_up, w_down):
    gate_act = jnp.einsum("erd,efd->erf", token_rows, w_gate, preferred_element_type=jnp.float32)
    up_act = jnp.einsum("erd,efd->erf", token_rows, w_up, preferred_element_type=jnp.float32)
    hidden = (jax.nn.silu(gate_act) * up_act).astype(jnp.bfloat16)
    expert_out = jnp.einsum("erf,efd->erd", hidden, w_down, preferred_element_type=jnp.float32)
    return (expert_out * weights.astype(jnp.float32)[..., None]).astype(jnp.bfloat16)


def body(tokens, expert_ids, route_logits, w_gate, w_up, w_down):
    route_probs = jax.nn.softmax(route_logits, axis=-1).astype(jnp.bfloat16)
    probs_wide = route_probs.astype(jnp.float32)
    numbers = jnp.arange(EXP_WIN, dtype=jnp.int32)
    chosen = expert_ids[:, :, None] == numbers[None, None, :]
    combine = jnp.sum(jnp.where(chosen, probs_wide[:, :, None], jnp.float32(0.0)), axis=1).astype(
        jnp.bfloat16
    )
    selector = slot_onehot(combine > 0, CAP)
    token_rows = jnp.einsum(
        "esr,rd->esd", selector, tokens, preferred_element_type=jnp.float32
    ).astype(jnp.bfloat16)
    weights = jnp.einsum(
        "esr,re->es", selector.astype(jnp.float32), combine.astype(jnp.float32)
    ).astype(jnp.bfloat16)
    all_rows, all_weights = (
        lax.all_gather(token_rows, "et", axis=1, tiled=True),
        lax.all_gather(weights, "et", axis=1, tiled=True),
    )
    partial_value = experts_apply(all_rows, all_weights, w_gate, w_up, w_down)
    own_sums = lax.psum_scatter(partial_value, "et", scatter_dimension=1, tiled=True).astype(
        jnp.float32
    )
    summed = jnp.einsum("esr,esd->rd", selector.astype(jnp.float32), own_sums)
    return summed.astype(jnp.bfloat16)


def solution(mesh):
    in_specs = (
        P(("rep", "et"), None),
        P(("rep", "et"), None),
        P(("rep", "et"), None),
        P(None, "et", None),
        P(None, "et", None),
        P(None, "et", None),
    )
    out_specs = P(("rep", "et"), None)
    return jax.shard_map(body, mesh=mesh, in_specs=in_specs, out_specs=out_specs, check_vma=False)
```

profile of v0, /device:TPU:0, one launch (start us, length us, event | category | flops | bytes accessed | tf_op | source)
XLA Modules:
  0.0 124.6 jit_solution(8226636055367859207)
XLA Ops:
  6.5 0.0 copy-start
  6.5 0.0 all-gather.3.cloned.1.call-start
  6.5 0.8 reduce_max.9
  7.3 0.7 fusion.10
  8.0 0.7 fusion.11
  8.7 0.7 fusion.7
  9.4 0.1 copy.26
  9.5 0.2 reduce_window_sum.11
  9.7 0.1 copy.27
  9.7 0.0 copy-done
  9.8 1.0 convolution_convert_fusion
  10.8 0.0 all-gather.3.cloned.1.call-update
  10.8 0.0 reduce-scatter.2.cloned.1.call-start
  10.8 0.1 fusion.3
  11.0 12.5 %all-gather = bf16[4,48,2]{1,2,0:T(2,128)(2,1)S(1)} all-gather(bf16[1,48,2]{1,2,0:T(2,128)(2,1)S(1)} %convert_bitcast_fusion), channel_id=1, replica_groups=mesh['rep'=8,'et'=4] {'et'}, dimensions={0}, use_global_device_ids=true | all-gather | bytes 960 | tf_op jit(solution)/shard_map/all_gather | solution.py:42
  23.5 0.1 reshape.8
  23.6 27.1 %all-gather.3.cloned.1.call-done = bf16[2,192,2048]{2,1,0:T(8,128)(2,1)} async-done(((bf16[2,48,2048]{2,1,0:T(8,128)(2,1)}), bf16[2,192,2048]{2,1,0:T(8,128)(2,1)}) %all-gather.3.cloned.1.call-update) | async-done | bytes 1572880 | tf_op jit(solution)/shard_map/all_gather | solution.py:41
  50.7 8.7 %fusion.12 = f32[2,192,1792]{2,1,0:T(8,128)S(1)} fusion(bf16[2,192,2048]{2,1,0:T(8,128)(2,1)} %all-gather.3.cloned.1.call-done, bf16[2,1792,2048]{2,1,0:T(8,128)(2,1)} %param.9), kind=kOutput, calls=%fused_computation.25 | convolution fusion | flops 2818572288 | bytes 19005440 | tf_op jit(solution)/shard_map/erd,efd->erf/dot_general | solution.py:18
  59.5 12.1 %fusion = bf16[2,192,1792]{2,1,0:T(8,128)(2,1)} fusion(bf16[2,192,2048]{2,1,0:T(8,128)(2,1)} %all-gather.3.cloned.1.call-done, bf16[2,1792,2048]{2,1,0:T(8,128)(2,1)} %param.10, f32[2,192,1792]{2,1,0:T(8,128)S(1)} %fusion.12), kind=kOutput, calls=%fused_computation.2 | convolution fusion | flops 2822701056 | bytes 20381696 | tf_op jit(solution)/shard_map/erd,efd->erf/dot_general | solution.py:19
  71.5 9.8 %multiply_convert_fusion = bf16[2,192,2048]{2,1,0:T(8,128)(2,1)} fusion(bf16[2,192,1792]{2,1,0:T(8,128)(2,1)} %fusion, bf16[2,1792,2048]{2,1,0:T(8,128)(2,1)} %param.11, f32[2,192]{1,0:T(2,128)S(1)} %bitcast.28), kind=kOutput, calls=%fused_computation | convolution fusion | flops 2820145152 | bytes 17630720 | tf_op jit(solution)/shard_map/erf,efd->erd/dot_general | solution.py:21
  81.3 0.0 reduce-scatter.2.cloned.1.call-update
  81.3 34.3 %reduce-scatter.2.cloned.1.call-done = bf16[2,48,2048]{2,1,0:T(8,128)(2,1)} async-done(((bf16[2,192,2048]{2,1,0:T(8,128)(2,1)}), bf16[2,48,2048]{2,1,0:T(8,128)(2,1)}) %reduce-scatter.2.cloned.1.call-update) | async-done | bytes 393232 | tf_op jit(solution)/shard_map/reduce_scatter | solution.py:45
  115.6 2.1 %fusion.1 = bf16[128,2048]{1,0:T(8,128)(2,1)} fusion(bf16[2,48,2048]{2,1,0:T(8,128)(2,1)} %reduce-scatter.2.cloned.1.call-done, s32[2,128]{1,0:T(2,128)S(1)} %fusion.8), kind=kOutput, calls=%fused_computation.4 | convolution fusion | flops 50606080 | bytes 918528 | tf_op jit(solution)/shard_map/esr,esd->rd/dot_general | solution.py:48
  (4 shorter events, 0.0 us)
Async XLA Ops:
  6.5 3.2 %copy-start = (bf16[128,2048]{1,0:T(8,128)(2,1)S(1)}, bf16[128,2048]{1,0:T(8,128)(2,1)}, u32[]{:S(2)}) copy-start(bf16[128,2048]{1,0:T(8,128)(2,1)} %param.6) | copy-start | bytes 1572868
  6.5 44.2 %all-gather.3.cloned.1.call-start = ((), (), s32[]{:S(2)}) async-start(), calls=%async_computation.1 | async-start | bytes 1966080 | tf_op jit(solution)/shard_map/all_gather | solution.py:41
  10.8 104.8 %reduce-scatter.2.cloned.1.call-start = ((), (), s32[]{:S(2)}) async-start(), calls=%async_computation.2 | async-start | bytes 1966080 | tf_op jit(solution)/shard_map/reduce_scatter | solution.py:45
Sparse Core Ops, SparseCore 0:
  10.9 39.7 all-gather.2
  81.4 34.1 reduce-scatter.1
where the time goes:
time: 125 us
  waiting for transfers between devices  61.5 us (49%)
  matrix products  33.8 us (27%)
  between operations  13.4 us (11%)
  blocking collectives  12.5 us (10%)
  other arithmetic  3.03 us (2%)
    reduce_scatter x1, waiting for transfers between devices, body(): lax.psum_scatter(partial_value, 'et', scatter_dimension=1, tiled=True)  34.3 us
    all_gather x1, waiting for transfers between devices, body(): lax.all_gather(token_rows, 'et', axis=1, tiled=True)  27.1 us
    all_gather x1, blocking collectives, body(): lax.all_gather(weights, 'et', axis=1, tiled=True)  12.5 us
    dot_general x1, matrix products, experts_apply(): jnp.einsum('erd,efd->erf', token_rows, w_up, preferred_element_type=jnp.f...  12.1 us
    dot_general x1, matrix products, experts_apply(): jnp.einsum('erf,efd->erd', hidden, w_down, preferred_element_type=jnp.flo...  9.78 us
    dot_general x1, matrix products, experts_apply(): jnp.einsum('erd,efd->erf', token_rows, w_gate, preferred_element_type=jnp...  8.7 us
  transfers between devices with their start and end apart: 2, of which 2 were waited for; matrix products, arithmetic and copies ran while one was open for 0% of the time, Pallas kernels for 0%

commit v1 on v0

v1 whole, which is shorter than its diff:
```python
import functools

import jax
import jax.numpy as jnp
from jax import lax
from jax.experimental import pallas as pl
from jax.experimental.pallas import tpu as pltpu
from jax.sharding import PartitionSpec as P

EXP_WIN = 2
CAP = 48
CHUNKS = ((0, 16), (0, 32), (1, 32), (1, 16))
F_TILE = 256
D_TILE = 512
MESH = pl.DeviceIdType.MESH


def chunk_starts():
    starts, seen = [], 0
    for _, rows in CHUNKS:
        starts.append(seen)
        seen += rows
    return starts


def routing(ids, logits):
    rows, slots = ids.shape[1], EXP_WIN * CAP
    low, high = logits[0:1, :], logits[1:2, :]
    top = jnp.maximum(low, high)
    exp_low, exp_high = jnp.exp(low - top), jnp.exp(high - top)
    total = exp_low + exp_high
    prob_low = (exp_low / total).astype(jnp.bfloat16).astype(jnp.float32)
    prob_high = (exp_high / total).astype(jnp.bfloat16).astype(jnp.float32)
    slot = lax.broadcasted_iota(jnp.int32, (slots, rows), 0)
    expert = jnp.where(slot >= CAP, 1, 0)
    in_low, in_high = ids[0:1, :] == expert, ids[1:2, :] == expert
    weight = jnp.where(in_low, prob_low, 0.0) + jnp.where(in_high, prob_high, 0.0)
    routed = jnp.where(in_low, 1.0, 0.0) + jnp.where(in_high, 1.0, 0.0)
    upper = lax.broadcasted_iota(jnp.int32, (rows, rows), 0) <= lax.broadcasted_iota(jnp.int32, (rows, rows), 1)
    ranking = jnp.dot(
        routed.astype(jnp.bfloat16), jnp.where(upper, 1.0, 0.0).astype(jnp.bfloat16), preferred_element_type=jnp.float32
    )
    place = (slot - CAP * expert + 1).astype(jnp.float32)
    selected = jnp.where(ranking == place, routed, 0.0)
    return selected.astype(jnp.bfloat16), (selected * weight).astype(jnp.bfloat16)


def kernel(n, tokens, ids, logits, w_gate, w_up, w_down, out, *scratch):
    count = len(CHUNKS)
    rows_of = scratch[0:count]
    term_of = scratch[count : 2 * count]
    right_of = scratch[2 * count : 3 * count]
    left_of = scratch[3 * count : 4 * count]
    gate, up, down, hidden, own, weighted, load_sem, ag_send, ag_recv, rs_send, rs_recv = scratch[4 * count :]
    p = lax.axis_index("et")
    features = tokens.shape[1]
    units = gate.shape[1]
    f_tile = F_TILE if units % F_TILE == 0 else units
    f_steps, d_steps = units // f_tile, features // D_TILE
    starts = chunk_starts()
    has_left, has_right = p > 0, p < n - 1

    def load(index, expert):
        source, held = ((w_gate, gate), (w_up, up), (w_down, down))[index]
        return pltpu.make_async_copy(source.at[expert], held.at[expert], load_sem.at[index, expert])

    for index in range(3):
        load(index, 0).start()

    barrier = pltpu.get_barrier_semaphore()

    @pl.when(has_left)
    def _():
        pl.semaphore_signal(barrier, inc=1, device_id={"et": p - 1}, device_id_type=MESH)

    @pl.when(has_right)
    def _():
        pl.semaphore_signal(barrier, inc=1, device_id={"et": p + 1}, device_id_type=MESH)

    plain, scaled = routing(ids[...], logits[...])
    weighted[...] = scaled
    for part in range(d_steps):
        columns = pl.ds(part * D_TILE, D_TILE)
        picked = jnp.dot(plain, tokens[:, columns], preferred_element_type=jnp.float32).astype(jnp.bfloat16)
        for c, (_, size) in enumerate(CHUNKS):
            rows_of[c][p, :, columns] = picked[starts[c] : starts[c] + size]

    pl.semaphore_wait(barrier, jnp.where(has_left & has_right, 2, 1))

    def ag_right(c, k):
        return pltpu.make_async_remote_copy(
            src_ref=rows_of[c].at[p - k],
            dst_ref=rows_of[c].at[p - k],
            send_sem=ag_send.at[0, c, k],
            recv_sem=ag_recv.at[0, c, k + 1],
            device_id={"et": p + 1},
            device_id_type=MESH,
        )

    def ag_left(c, k):
        return pltpu.make_async_remote_copy(
            src_ref=rows_of[c].at[p + k],
            dst_ref=rows_of[c].at[p + k],
            send_sem=ag_send.at[1, c, k],
            recv_sem=ag_recv.at[1, c, k + 1],
            device_id={"et": p - 1},
            device_id_type=MESH,
        )

    def ag_wait(c, k):
        @pl.when(p - k >= 0)
        def _():
            pltpu.make_async_remote_copy(
                src_ref=rows_of[c].at[p - k],
                dst_ref=rows_of[c].at[p - k],
                send_sem=ag_send.at[0, c, k - 1],
                recv_sem=ag_recv.at[0, c, k],
                device_id={"et": p - 1},
                device_id_type=MESH,
            ).wait_recv()

        @pl.when(p + k <= n - 1)
        def _():
            pltpu.make_async_remote_copy(
                src_ref=rows_of[c].at[p + k],
                dst_ref=rows_of[c].at[p + k],
                send_sem=ag_send.at[1, c, k - 1],
                recv_sem=ag_recv.at[1, c, k],
                device_id={"et": p + 1},
                device_id_type=MESH,
            ).wait_recv()

    def ag_each(c, k, act):
        @pl.when((p - k >= 0) & has_right)
        def _():
            act(ag_right(c, k))

        @pl.when((p + k <= n - 1) & has_left)
        def _():
            act(ag_left(c, k))

    def gather(c, k):
        if k > 0:
            ag_wait(c, k)
        if k < n - 1:
            ag_each(c, k, lambda copy: copy.start())

    def rs_copy(c, k, way):
        held = (right_of, left_of)[way][c]
        return pltpu.make_async_remote_copy(
            src_ref=held.at[k],
            dst_ref=held.at[k - 1],
            send_sem=rs_send.at[way, c, k],
            recv_sem=rs_recv.at[way, c, k - 1],
            device_id={"et": p + 1 if way == 0 else p - 1},
            device_id_type=MESH,
        )

    def rs_wait(c, k, way):
        held = (right_of, left_of)[way][c]
        pltpu.make_async_remote_copy(
            src_ref=held.at[k + 1],
            dst_ref=held.at[k],
            send_sem=rs_send.at[way, c, k + 1],
            recv_sem=rs_recv.at[way, c, k],
            device_id={"et": p - 1 if way == 0 else p + 1},
            device_id_type=MESH,
        ).wait_recv()

    def rs_step(c, k):
        for way in range(2):
            held = (right_of, left_of)[way][c]
            target = p + k if way == 0 else p - k
            exists = target <= n - 1 if way == 0 else target >= 0
            behind = has_left if way == 0 else has_right
            if k < n - 1:

                @pl.when(exists & behind)
                def _():
                    rs_wait(c, k, way)
                    held[k] = (held[k].astype(jnp.float32) + term_of[c][target].astype(jnp.float32)).astype(jnp.bfloat16)

            @pl.when(exists & jnp.logical_not(behind))
            def _():
                held[k] = term_of[c][target]

            @pl.when(exists)
            def _():
                rs_copy(c, k, way).start()

    def gate_up(c, first, last):
        expert, size = CHUNKS[c]
        m = n * size

        @pl.loop(first, last)
        def _(i):
            at = pl.ds(pl.multiple_of(i * f_tile, f_tile), f_tile)
            x = rows_of[c][...].reshape(m, features)
            dims = (((1,), (1,)), ((), ()))
            g = lax.dot_general(x, gate[expert, at, :], dims, preferred_element_type=jnp.float32)
            u = lax.dot_general(x, up[expert, at, :], dims, preferred_element_type=jnp.float32)
            hidden[0:m, at] = (g / (1.0 + jnp.exp(-g)) * u).astype(jnp.bfloat16)

    def project(c, first, last):
        expert, size = CHUNKS[c]
        m = n * size

        @pl.loop(first, last)
        def _(j):
            at = pl.ds(pl.multiple_of(j * D_TILE, D_TILE), D_TILE)
            y = jnp.dot(hidden[0:m, :], down[expert, :, at], preferred_element_type=jnp.float32)
            term_of[c][:, :, at] = y.astype(jnp.bfloat16).reshape(n, size, D_TILE)

    for k in range(n):
        gather(0, k)
        if k == n - 2 and count > 1:
            gather(1, 0)

    for c, (expert, size) in enumerate(CHUNKS):
        first_use = c == 0 or CHUNKS[c - 1][0] != expert
        pieces = []
        half = f_steps // 2
        if half > 0:
            pieces.append(functools.partial(gate_up, c, 0, half))
        pieces.append(functools.partial(gate_up, c, half, f_steps))
        pieces.append(functools.partial(project, c, 0, d_steps // 2))
        pieces.append(functools.partial(project, c, d_steps // 2, d_steps))
        services = []
        for k in range(1, n - 1):
            if c + 1 < count:
                services.append(functools.partial(gather, c + 1, k))
            if c > 0:
                services.append(functools.partial(rs_step, c - 1, n - 1 - k))
        if c + 2 < count:
            services.append(functools.partial(gather, c + 2, 0))
        if first_use:
            load(0, expert).wait()
            load(1, expert).wait()
        if c == 0:
            for index in range(3):
                load(index, 1).start()
        done = 0
        for i, piece in enumerate(pieces):
            if first_use and i == len(pieces) - 2:
                load(2, expert).wait()
            piece()
            upto = (i + 1) * len(services) // len(pieces)
            for service in services[done:upto]:
                service()
            done = upto
        rs_step(c, n - 1)
        if c + 1 < count:
            gather(c + 1, n - 1)
    for k in range(n - 2, 0, -1):
        rs_step(count - 1, k)

    for c, (_, size) in enumerate(CHUNKS):
        at = pl.ds(starts[c], size)
        own[at, :] = term_of[c][p]

        @pl.when(has_left)
        def _():
            rs_wait(c, 0, 0)

        @pl.when(has_right)
        def _():
            rs_wait(c, 0, 1)

        @pl.when(has_left & has_right)
        def _():
            total = right_of[c][0].astype(jnp.float32) + left_of[c][0].astype(jnp.float32)
            own[at, :] = (total + term_of[c][p].astype(jnp.float32)).astype(jnp.bfloat16)

        @pl.when(has_left & jnp.logical_not(has_right))
        def _():
            own[at, :] = (right_of[c][0].astype(jnp.float32) + term_of[c][p].astype(jnp.float32)).astype(jnp.bfloat16)

        @pl.when(has_right & jnp.logical_not(has_left))
        def _():
            own[at, :] = (left_of[c][0].astype(jnp.float32) + term_of[c][p].astype(jnp.float32)).astype(jnp.bfloat16)

    for part in range(d_steps):
        columns = pl.ds(part * D_TILE, D_TILE)
        mixed = lax.dot_general(
            weighted[...], own[:, columns], (((0,), (0,)), ((), ())), preferred_element_type=jnp.float32
        )
        out[:, columns] = mixed.astype(jnp.bfloat16)

    for c in range(count):
        for k in range(n - 1):
            ag_each(c, k, lambda copy: copy.wait_send())
        for k in range(1, n):

            @pl.when(p + k <= n - 1)
            def _():
                rs_copy(c, k, 0).wait_send()

            @pl.when(p - k >= 0)
            def _():
                rs_copy(c, k, 1).wait_send()


def body(n, tokens, expert_ids, route_logits, w_gate, w_up, w_down):
    count, features, units = len(CHUNKS), tokens.shape[1], w_gate.shape[1]
    most = max(size for _, size in CHUNKS)
    per_chunk = [pltpu.VMEM((n, size, features), jnp.bfloat16) for _, size in CHUNKS]
    vmem = pl.BlockSpec(memory_space=pltpu.VMEM)
    hbm = pl.BlockSpec(memory_space=pl.ANY)
    weights = pltpu.VMEM((EXP_WIN, units, features), jnp.bfloat16)
    return pl.pallas_call(
        functools.partial(kernel, n),
        out_shape=jax.ShapeDtypeStruct(tokens.shape, jnp.bfloat16),
        in_specs=[vmem, vmem, vmem, hbm, hbm, hbm],
        out_specs=vmem,
        scratch_shapes=per_chunk * 4
        + [
            weights,
            weights,
            weights,
            pltpu.VMEM((n * most, units), jnp.bfloat16),
            pltpu.VMEM((EXP_WIN * CAP, features), jnp.bfloat16),
            pltpu.VMEM((EXP_WIN * CAP, tokens.shape[0]), jnp.bfloat16),
            pltpu.SemaphoreType.DMA((3, EXP_WIN)),
            pltpu.SemaphoreType.DMA((2, count, n)),
            pltpu.SemaphoreType.DMA((2, count, n)),
            pltpu.SemaphoreType.DMA((2, count, n)),
            pltpu.SemaphoreType.DMA((2, count, n)),
        ],
        compiler_params=pltpu.CompilerParams(collective_id=0, has_side_effects=True, vmem_limit_bytes=60 * 2**20),
    )(tokens, expert_ids.T, route_logits.T, w_gate, w_up, w_down)


def solution(mesh):
    in_specs = (
        P(("rep", "et"), None),
        P(("rep", "et"), None),
        P(("rep", "et"), None),
        P(None, "et", None),
        P(None, "et", None),
        P(None, "et", None),
    )
    out_specs = P(("rep", "et"), None)
    return jax.shard_map(
        functools.partial(body, mesh.shape["et"]), mesh=mesh, in_specs=in_specs, out_specs=out_specs, check_vma=False
    )
```

time: 125 us -> 72.4 us (0.58)
  Pallas kernels: 0 us -> 70.3 us
  waiting for transfers between devices: 61.5 us -> 0 us
  matrix products: 33.8 us -> 0 us
  between operations: 13.4 us -> 0.01 us
  blocking collectives: 12.5 us -> 0 us
  other arithmetic: 3.03 us -> 0 us
  local copies, waits for them, and re-layouts: 0.27 us -> 1.88 us
    pallas_call x0 -> x1, Pallas kernels: none -> 70.3 us  [body(): pl.pallas_call(functools.partial(kernel, n), out_shape=jax.ShapeDtypeStru...]
    reduce_scatter x1 -> x0, waiting for transfers between devices: 34.3 us -> none  [body(): lax.psum_scatter(partial_value, 'et', scatter_dimension=1, tiled=True)]
    dot_general x6 -> x0, matrix products: 33.8 us -> none  [the longest x1 12.1 us: experts_apply(): jnp.einsum('erd,efd->erf', token_rows, w_up, preferred_element_type=jnp.f...]
    all_gather x1 -> x0, waiting for transfers between devices: 27.1 us -> none  [body(): lax.all_gather(token_rows, 'et', axis=1, tiled=True)]
    all_gather x1 -> x0, blocking collectives: 12.5 us -> none  [body(): lax.all_gather(weights, 'et', axis=1, tiled=True)]
    unnamed x2 -> x1, local copies, waits for them, and re-layouts: 0.01 us -> 1.88 us
    reduce_sum x2 -> x0, other arithmetic: 1.39 us -> none  [the longest x1 0.7 us: body(): jnp.sum(jnp.where(chosen, probs_wide[:, :, None], jnp.float32(0.0)), axis=1)]
  transfers between devices with their start and end apart: 2 -> 0, of which waited for: 2 -> 0; matrix products, arithmetic and copies ran while one was open for 0% -> 0% of each run, Pallas kernels for 0% -> 0%
where the time goes in v1:
time: 72.4 us; the launch traced here: 72.2 us
  Pallas kernels  70.3 us (97%)
  local copies, waits for them, and re-layouts  1.88 us (3%)
    pallas_call x1, Pallas kernels, body(): pl.pallas_call(functools.partial(kernel, n), out_shape=jax.ShapeDtypeStru...  70.3 us
    unnamed x1, local copies, waits for them, and re-layouts  1.88 us

profile of v1, /device:TPU:0, one launch (start us, length us, event | category | flops | bytes accessed | tf_op | source)
XLA Modules:
  0.0 72.2 jit_solution(13457648248624710007)
XLA Ops:
  0.0 70.3 %shard_map.64 = bf16[128,2048]{1,0:T(8,128)(2,1)} custom-call(bf16[128,2048]{1,0:T(8,128)(2,1)} %tokens.1, s32[2,128]{1,0:T(2,128)} %bitcast.2, f32[2,128]{1,0:T(2,128)} %bitcast.3, bf16[2,1792,2048]{2,1,0:T(8,128)(2,1)} %w_gate.1, bf16[2,1792,2048]{2,1,0:T(8,128)(2,1)} %w_up.1, bf16[2,1792,2048]{2,1,0:T(8,128)(2,1)} %w_down.1), custom_call_target="tpu_custom_call" | custom-call | tf_op jit(solution)/shard_map/pallas_call | solution.py:310
  70.3 1.9 %copy.8 = bf16[128,2048]{1,0:T(8,128)(2,1)} copy(bf16[128,2048]{1,0:T(8,128)(2,1)} %shard_map.64) | data formatting | bytes 1048576

commit v2 on v1

--- a/solution.py
+++ b/solution.py
@@ -9,7 +9,7 @@
 
 EXP_WIN = 2
 CAP = 48
-CHUNKS = ((0, 16), (0, 32), (1, 32), (1, 16))
+CHUNKS = ((0, 48), (1, 48))
 F_TILE = 256
 D_TILE = 512
 MESH = pl.DeviceIdType.MESH

time: 72.4 us -> 68.2 us (0.942)
  Pallas kernels: 70.3 us -> 66.1 us
    pallas_call x1, Pallas kernels: 70.3 us -> 66.1 us  [body(): pl.pallas_call(functools.partial(kernel, n), out_shape=jax.ShapeDtypeStru...]
where the time goes in v2:
time: 68.2 us; the launch traced here: 68 us
  Pallas kernels  66.1 us (97%)
  local copies, waits for them, and re-layouts  1.88 us (3%)
    pallas_call x1, Pallas kernels, body(): pl.pallas_call(functools.partial(kernel, n), out_shape=jax.ShapeDtypeStru...  66.1 us
    unnamed x1, local copies, waits for them, and re-layouts  1.88 us

profile of v2, /device:TPU:0, one launch (start us, length us, event | category | flops | bytes accessed | tf_op | source)
XLA Modules:
  0.0 68.0 jit_solution(2446779683709059541)
XLA Ops:
  0.0 66.1 %shard_map.64 = bf16[128,2048]{1,0:T(8,128)(2,1)} custom-call(bf16[128,2048]{1,0:T(8,128)(2,1)} %tokens.1, s32[2,128]{1,0:T(2,128)} %bitcast.2, f32[2,128]{1,0:T(2,128)} %bitcast.3, bf16[2,1792,2048]{2,1,0:T(8,128)(2,1)} %w_gate.1, bf16[2,1792,2048]{2,1,0:T(8,128)(2,1)} %w_up.1, bf16[2,1792,2048]{2,1,0:T(8,128)(2,1)} %w_down.1), custom_call_target="tpu_custom_call" | custom-call | tf_op jit(solution)/shard_map/pallas_call | solution.py:310
  66.2 1.9 %copy.8 = bf16[128,2048]{1,0:T(8,128)(2,1)} copy(bf16[128,2048]{1,0:T(8,128)(2,1)} %shard_map.64) | data formatting | bytes 1048576

commit v3 on v2

--- a/solution.py
+++ b/solution.py
@@ -51,7 +51,7 @@
     term_of = scratch[count : 2 * count]
     right_of = scratch[2 * count : 3 * count]
     left_of = scratch[3 * count : 4 * count]
-    gate, up, down, hidden, own, weighted, load_sem, ag_send, ag_recv, rs_send, rs_recv = scratch[4 * count :]
+    gate, up, down, turned, hidden, own, weighted, load_sem, ag_send, ag_recv, rs_send, rs_recv = scratch[4 * count :]
     p = lax.axis_index("et")
     features = tokens.shape[1]
     units = gate.shape[1]
@@ -188,6 +188,15 @@
             def _():
                 rs_copy(c, k, way).start()
 
+    def turn(c):
+        size = CHUNKS[c][1]
+        m = n * size
+
+        @pl.loop(0, d_steps)
+        def _(j):
+            at = pl.ds(pl.multiple_of(j * D_TILE, D_TILE), D_TILE)
+            turned[at, 0:m] = rows_of[c][:, :, at].reshape(m, D_TILE).T
+
     def gate_up(c, first, last):
         expert, size = CHUNKS[c]
         m = n * size
@@ -195,11 +204,10 @@
         @pl.loop(first, last)
         def _(i):
             at = pl.ds(pl.multiple_of(i * f_tile, f_tile), f_tile)
-            x = rows_of[c][...].reshape(m, features)
-            dims = (((1,), (1,)), ((), ()))
-            g = lax.dot_general(x, gate[expert, at, :], dims, preferred_element_type=jnp.float32)
-            u = lax.dot_general(x, up[expert, at, :], dims, preferred_element_type=jnp.float32)
-            hidden[0:m, at] = (g / (1.0 + jnp.exp(-g)) * u).astype(jnp.bfloat16)
+            x = turned[:, 0:m]
+            g = jnp.dot(gate[expert, at, :], x, preferred_element_type=jnp.float32)
+            u = jnp.dot(up[expert, at, :], x, preferred_element_type=jnp.float32)
+            hidden[0:m, at] = (g / (1.0 + jnp.exp(-g)) * u).T.astype(jnp.bfloat16)
 
     def project(c, first, last):
         expert, size = CHUNKS[c]
@@ -218,6 +226,7 @@
 
     for c, (expert, size) in enumerate(CHUNKS):
         first_use = c == 0 or CHUNKS[c - 1][0] != expert
+        turn(c)
         pieces = []
         half = f_steps // 2
         if half > 0:
@@ -317,6 +326,7 @@
             weights,
             weights,
             weights,
+            pltpu.VMEM((features, n * most), jnp.bfloat16),
             pltpu.VMEM((n * most, units), jnp.bfloat16),
             pltpu.VMEM((EXP_WIN * CAP, features), jnp.bfloat16),
             pltpu.VMEM((EXP_WIN * CAP, tokens.shape[0]), jnp.bfloat16),

time: 68.2 us -> 68.3 us (level)
  no operation moved by 1% of the time
where the time goes in v3:
time: 68.3 us; the launch traced here: 68.2 us
  Pallas kernels  66.3 us (97%)
  local copies, waits for them, and re-layouts  1.88 us (3%)
    pallas_call x1, Pallas kernels, body(): pl.pallas_call(functools.partial(kernel, n), out_shape=jax.ShapeDtypeStru...  66.3 us
    unnamed x1, local copies, waits for them, and re-layouts  1.88 us

profile of v3, /device:TPU:0, one launch (start us, length us, event | category | flops | bytes accessed | tf_op | source)
XLA Modules:
  0.0 68.2 jit_solution(191566484293032074)
XLA Ops:
  0.0 66.3 %shard_map.64 = bf16[128,2048]{1,0:T(8,128)(2,1)} custom-call(bf16[128,2048]{1,0:T(8,128)(2,1)} %tokens.1, s32[2,128]{1,0:T(2,128)} %bitcast.2, f32[2,128]{1,0:T(2,128)} %bitcast.3, bf16[2,1792,2048]{2,1,0:T(8,128)(2,1)} %w_gate.1, bf16[2,1792,2048]{2,1,0:T(8,128)(2,1)} %w_up.1, bf16[2,1792,2048]{2,1,0:T(8,128)(2,1)} %w_down.1), custom_call_target="tpu_custom_call" | custom-call | tf_op jit(solution)/shard_map/pallas_call | solution.py:319
  66.3 1.9 %copy.8 = bf16[128,2048]{1,0:T(8,128)(2,1)} copy(bf16[128,2048]{1,0:T(8,128)(2,1)} %shard_map.64) | data formatting | bytes 1048576

commit v4 on v1

--- a/solution.py
+++ b/solution.py
@@ -10,6 +10,7 @@
 EXP_WIN = 2
 CAP = 48
 CHUNKS = ((0, 16), (0, 32), (1, 32), (1, 16))
+UNIT = 16
 F_TILE = 256
 D_TILE = 512
 MESH = pl.DeviceIdType.MESH
@@ -45,19 +46,20 @@
     return selected.astype(jnp.bfloat16), (selected * weight).astype(jnp.bfloat16)
 
 
-def kernel(n, tokens, ids, logits, w_gate, w_up, w_down, out, *scratch):
+def kernel(n, tokens, ids, logits, w_gate, w_up, w_down, own, weighted, *scratch):
     count = len(CHUNKS)
     rows_of = scratch[0:count]
     term_of = scratch[count : 2 * count]
     right_of = scratch[2 * count : 3 * count]
     left_of = scratch[3 * count : 4 * count]
-    gate, up, down, hidden, own, weighted, load_sem, ag_send, ag_recv, rs_send, rs_recv = scratch[4 * count :]
+    gate, up, down, hidden, load_sem, ag_send, ag_recv, rs_send, rs_recv = scratch[4 * count :]
     p = lax.axis_index("et")
     features = tokens.shape[1]
     units = gate.shape[1]
     f_tile = F_TILE if units % F_TILE == 0 else units
     f_steps, d_steps = units // f_tile, features // D_TILE
     starts = chunk_starts()
+    units_of = [(c, at) for c, (_, size) in enumerate(CHUNKS) for at in range(0, size, UNIT)]
     has_left, has_right = p > 0, p < n - 1
 
     def load(index, expert):
@@ -87,63 +89,42 @@
 
     pl.semaphore_wait(barrier, jnp.where(has_left & has_right, 2, 1))
 
-    def ag_right(c, k):
+    def ag_copy(u, k, way, arriving=False):
+        c, at = units_of[u]
+        source = p - k if way == 0 else p + k
+        held = rows_of[c].at[source, pl.ds(at, UNIT)]
+        step = k - 1 if arriving else k
         return pltpu.make_async_remote_copy(
-            src_ref=rows_of[c].at[p - k],
-            dst_ref=rows_of[c].at[p - k],
-            send_sem=ag_send.at[0, c, k],
-            recv_sem=ag_recv.at[0, c, k + 1],
-            device_id={"et": p + 1},
+            src_ref=held,
+            dst_ref=held,
+            send_sem=ag_send.at[way, u, step],
+            recv_sem=ag_recv.at[way, u, step + 1],
+            device_id={"et": p + 1 if (way == 0) != arriving else p - 1},
             device_id_type=MESH,
         )
 
-    def ag_left(c, k):
-        return pltpu.make_async_remote_copy(
-            src_ref=rows_of[c].at[p + k],
-            dst_ref=rows_of[c].at[p + k],
-            send_sem=ag_send.at[1, c, k],
-            recv_sem=ag_recv.at[1, c, k + 1],
-            device_id={"et": p - 1},
-            device_id_type=MESH,
-        )
-
-    def ag_wait(c, k):
-        @pl.when(p - k >= 0)
-        def _():
-            pltpu.make_async_remote_copy(
-                src_ref=rows_of[c].at[p - k],
-                dst_ref=rows_of[c].at[p - k],
-                send_sem=ag_send.at[0, c, k - 1],
-                recv_sem=ag_recv.at[0, c, k],
-                device_id={"et": p - 1},
-                device_id_type=MESH,
-            ).wait_recv()
-
-        @pl.when(p + k <= n - 1)
-        def _():
-            pltpu.make_async_remote_copy(
-                src_ref=rows_of[c].at[p + k],
-                dst_ref=rows_of[c].at[p + k],
-                send_sem=ag_send.at[1, c, k - 1],
-                recv_sem=ag_recv.at[1, c, k],
-                device_id={"et": p + 1},
-                device_id_type=MESH,
-            ).wait_recv()
-
-    def ag_each(c, k, act):
+    def ag_each(u, k, act):
         @pl.when((p - k >= 0) & has_right)
         def _():
-            act(ag_right(c, k))
+            act(ag_copy(u, k, 0))
 
         @pl.when((p + k <= n - 1) & has_left)
         def _():
-            act(ag_left(c, k))
-
-    def gather(c, k):
+            act(ag_copy(u, k, 1))
+
+    def gather(u, k):
         if k > 0:
-            ag_wait(c, k)
+
+            @pl.when(p - k >= 0)
+            def _():
+                ag_copy(u, k, 0, True).wait_recv()
+
+            @pl.when(p + k <= n - 1)
+            def _():
+                ag_copy(u, k, 1, True).wait_recv()
+
         if k < n - 1:
-            ag_each(c, k, lambda copy: copy.start())
+            ag_each(u, k, lambda copy: copy.start())
 
     def rs_copy(c, k, way):
         held = (right_of, left_of)[way][c]
@@ -211,28 +192,22 @@
             y = jnp.dot(hidden[0:m, :], down[expert, :, at], preferred_element_type=jnp.float32)
             term_of[c][:, :, at] = y.astype(jnp.bfloat16).reshape(n, size, D_TILE)
 
-    for k in range(n):
-        gather(0, k)
-        if k == n - 2 and count > 1:
-            gather(1, 0)
+    events = sorted(((n - 1) * u + (k if k > 0 else -1), u, k) for u in range(len(units_of)) for k in range(n))
+    ready = [max(i for i, (_, u, _) in enumerate(events) if units_of[u][0] == c) + 1 for c in range(count)]
+    for _, u, k in events[: ready[0]]:
+        gather(u, k)
 
     for c, (expert, size) in enumerate(CHUNKS):
         first_use = c == 0 or CHUNKS[c - 1][0] != expert
-        pieces = []
-        half = f_steps // 2
-        if half > 0:
-            pieces.append(functools.partial(gate_up, c, 0, half))
-        pieces.append(functools.partial(gate_up, c, half, f_steps))
-        pieces.append(functools.partial(project, c, 0, d_steps // 2))
-        pieces.append(functools.partial(project, c, d_steps // 2, d_steps))
+        pieces = [functools.partial(gate_up, c, i, i + 1) for i in range(f_steps)]
+        pieces += [functools.partial(project, c, i, i + 1) for i in range(d_steps)]
         services = []
-        for k in range(1, n - 1):
-            if c + 1 < count:
-                services.append(functools.partial(gather, c + 1, k))
-            if c > 0:
-                services.append(functools.partial(rs_step, c - 1, n - 1 - k))
-        if c + 2 < count:
-            services.append(functools.partial(gather, c + 2, 0))
+        if c + 1 < count:
+            own_events = events[ready[c] : ready[c + 1]]
+            services += [((i + 1) / (len(own_events) + 1), 1, i, functools.partial(gather, u, k)) for i, (_, u, k) in enumerate(own_events)]
+        if c > 0:
+            services += [(i / (n - 1), 0, i, functools.partial(rs_step, c - 1, n - 1 - i)) for i in range(1, n - 1)]
+        services.sort(key=lambda entry: entry[:3])
         if first_use:
             load(0, expert).wait()
             load(1, expert).wait()
@@ -241,16 +216,15 @@
                 load(index, 1).start()
         done = 0
         for i, piece in enumerate(pieces):
-            if first_use and i == len(pieces) - 2:
+            if first_use and i == f_steps:
                 load(2, expert).wait()
             piece()
-            upto = (i + 1) * len(services) // len(pieces)
-            for service in services[done:upto]:
-                service()
-            done = upto
+            while done < len(services) and services[done][0] * len(pieces) <= i + 1:
+                services[done][3]()
+                done += 1
         rs_step(c, n - 1)
-        if c + 1 < count:
-            gather(c + 1, n - 1)
+        for entry in services[done:]:
+            entry[3]()
     for k in range(n - 2, 0, -1):
         rs_step(count - 1, k)
 
@@ -279,16 +253,10 @@
         def _():
             own[at, :] = (left_of[c][0].astype(jnp.float32) + term_of[c][p].astype(jnp.float32)).astype(jnp.bfloat16)
 
-    for part in range(d_steps):
-        columns = pl.ds(part * D_TILE, D_TILE)
-        mixed = lax.dot_general(
-            weighted[...], own[:, columns], (((0,), (0,)), ((), ())), preferred_element_type=jnp.float32
-        )
-        out[:, columns] = mixed.astype(jnp.bfloat16)
-
+    for u in range(len(units_of)):
+        for k in range(n - 1):
+            ag_each(u, k, lambda copy: copy.wait_send())
     for c in range(count):
-        for k in range(n - 1):
-            ag_each(c, k, lambda copy: copy.wait_send())
         for k in range(1, n):
 
             @pl.when(p + k <= n - 1)
@@ -302,32 +270,36 @@
 
 def body(n, tokens, expert_ids, route_logits, w_gate, w_up, w_down):
     count, features, units = len(CHUNKS), tokens.shape[1], w_gate.shape[1]
+    unit_count = sum(size // UNIT for _, size in CHUNKS)
     most = max(size for _, size in CHUNKS)
     per_chunk = [pltpu.VMEM((n, size, features), jnp.bfloat16) for _, size in CHUNKS]
     vmem = pl.BlockSpec(memory_space=pltpu.VMEM)
     hbm = pl.BlockSpec(memory_space=pl.ANY)
     weights = pltpu.VMEM((EXP_WIN, units, features), jnp.bfloat16)
-    return pl.pallas_call(
+    own, weighted = pl.pallas_call(
         functools.partial(kernel, n),
-        out_shape=jax.ShapeDtypeStruct(tokens.shape, jnp.bfloat16),
+        out_shape=(
+            jax.ShapeDtypeStruct((EXP_WIN * CAP, features), jnp.bfloat16),
+            jax.ShapeDtypeStruct((EXP_WIN * CAP, tokens.shape[0]), jnp.bfloat16),
+        ),
         in_specs=[vmem, vmem, vmem, hbm, hbm, hbm],
-        out_specs=vmem,
+        out_specs=(vmem, vmem),
         scratch_shapes=per_chunk * 4
         + [
             weights,
             weights,
             weights,
             pltpu.VMEM((n * most, units), jnp.bfloat16),
-            pltpu.VMEM((EXP_WIN * CAP, features), jnp.bfloat16),
-            pltpu.VMEM((EXP_WIN * CAP, tokens.shape[0]), jnp.bfloat16),
             pltpu.SemaphoreType.DMA((3, EXP_WIN)),
-            pltpu.SemaphoreType.DMA((2, count, n)),
-            pltpu.SemaphoreType.DMA((2, count, n)),
+            pltpu.SemaphoreType.DMA((2, unit_count, n)),
+            pltpu.SemaphoreType.DMA((2, unit_count, n)),
             pltpu.SemaphoreType.DMA((2, count, n)),
             pltpu.SemaphoreType.DMA((2, count, n)),
         ],
         compiler_params=pltpu.CompilerParams(collective_id=0, has_side_effects=True, vmem_limit_bytes=60 * 2**20),
     )(tokens, expert_ids.T, route_logits.T, w_gate, w_up, w_down)
+    mixed = lax.dot_general(weighted, own, (((0,), (0,)), ((), ())), preferred_element_type=jnp.float32)
+    return mixed.astype(jnp.bfloat16)
 
 
 def solution(mesh):

time: 72.4 us -> 81.4 us (1.12)
  Pallas kernels: 70.3 us -> 79.1 us
  matrix products: 0 us -> 2.13 us
  local copies, waits for them, and re-layouts: 1.88 us -> 0 us
    pallas_call x1, Pallas kernels: 70.3 us -> 79.1 us  [body(): pl.pallas_call(functools.partial(kernel, n), out_shape=(jax.ShapeDtypeStr...]
    dot_general x0 -> x1, matrix products: none -> 2.13 us  [body(): lax.dot_general(weighted, own, (((0,), (0,)), ((), ())), preferred_elemen...]
    unnamed x1 -> x0, local copies, waits for them, and re-layouts: 1.88 us -> none
where the time goes in v4:
time: 81.4 us; the launch traced here: 81.2 us
  Pallas kernels  79.1 us (97%)
  matrix products  2.13 us (3%)
    pallas_call x1, Pallas kernels, body(): pl.pallas_call(functools.partial(kernel, n), out_shape=(jax.ShapeDtypeStr...  79.1 us
    dot_general x1, matrix products, body(): lax.dot_general(weighted, own, (((0,), (0,)), ((), ())), preferred_elemen...  2.13 us

profile of v4, /device:TPU:0, one launch (start us, length us, event | category | flops | bytes accessed | tf_op | source)
XLA Modules:
  0.0 81.2 jit_solution(8542432095382277581)
XLA Ops:
  0.0 79.1 %shard_map.64 = (bf16[96,2048]{1,0:T(8,128)(2,1)}, bf16[96,128]{1,0:T(8,128)(2,1)}) custom-call(bf16[128,2048]{1,0:T(8,128)(2,1)} %tokens.1, s32[2,128]{1,0:T(2,128)} %bitcast.4, f32[2,128]{1,0:T(2,128)} %bitcast.5, bf16[2,1792,2048]{2,1,0:T(8,128)(2,1)} %w_gate.1, bf16[2,1792,2048]{2,1,0:T(8,128)(2,1)} %w_up.1, bf16[2,1792,2048]{2,1,0:T(8,128)(2,1)} %w_down.1), custom_call_target="tpu_custom_call" | custom-call | tf_op jit(solution)/shard_map/pallas_call | solution.py:279
  79.1 2.1 %convolution_convert_fusion = bf16[128,2048]{1,0:T(8,128)(2,1)} fusion(bf16[96,128]{1,0:T(8,128)(2,1)} %get-tuple-element.7, bf16[96,2048]{1,0:T(8,128)(2,1)} %get-tuple-element.8), kind=kOutput, calls=%fused_computation | convolution fusion | flops 50593792 | bytes 942080 | tf_op jit(solution)/shard_map/dot_general | solution.py:301

commit v5 on v0

v5 whole, which is shorter than its diff:
```python
import functools

import jax
import jax.numpy as jnp
from jax import lax
from jax.experimental import pallas as pl
from jax.experimental.pallas import tpu as pltpu
from jax.sharding import PartitionSpec as P

EXP_WIN = 2
CAP = 48
ROWS = 48
UNIT = 16
F_TILE = 256
D_TILE = 512
AG_INSIDE = 5
MESH = pl.DeviceIdType.MESH


def routing(ids, logits):
    rows, slots = ids.shape[1], EXP_WIN * CAP
    low, high = logits[0:1, :], logits[1:2, :]
    top = jnp.maximum(low, high)
    exp_low, exp_high = jnp.exp(low - top), jnp.exp(high - top)
    total = exp_low + exp_high
    prob_low = (exp_low / total).astype(jnp.bfloat16).astype(jnp.float32)
    prob_high = (exp_high / total).astype(jnp.bfloat16).astype(jnp.float32)
    slot = lax.broadcasted_iota(jnp.int32, (slots, rows), 0)
    expert = jnp.where(slot >= CAP, 1, 0)
    in_low, in_high = ids[0:1, :] == expert, ids[1:2, :] == expert
    weight = jnp.where(in_low, prob_low, 0.0) + jnp.where(in_high, prob_high, 0.0)
    routed = jnp.where(in_low, 1.0, 0.0) + jnp.where(in_high, 1.0, 0.0)
    upper = lax.broadcasted_iota(jnp.int32, (rows, rows), 0) <= lax.broadcasted_iota(jnp.int32, (rows, rows), 1)
    ranking = jnp.dot(
        routed.astype(jnp.bfloat16), jnp.where(upper, 1.0, 0.0).astype(jnp.bfloat16), preferred_element_type=jnp.float32
    )
    place = (slot - CAP * expert + 1).astype(jnp.float32)
    selected = jnp.where(ranking == place, routed, 0.0)
    return selected.astype(jnp.bfloat16), (selected * weight).astype(jnp.bfloat16)


def kernel(n, tokens, ids, logits, w_gate, w_up, w_down, own, weighted, *scratch):
    rows, terms, right, left, gate, up, down, hidden, total, load_sem, ag_send, ag_recv, rs_send, rs_recv = scratch
    p = lax.axis_index("et")
    features, units = tokens.shape[1], gate.shape[1]
    count, parts = EXP_WIN * CAP // ROWS, ROWS // UNIT
    per_expert = CAP // ROWS
    m = n * ROWS
    f_tile = F_TILE if units % F_TILE == 0 else units
    f_steps, d_steps = units // f_tile, features // D_TILE
    steps = f_steps + d_steps
    has_left, has_right = p > 0, p < n - 1

    def load(index, expert):
        source, held = ((w_gate, gate), (w_up, up), (w_down, down))[index]
        return pltpu.make_async_copy(source.at[expert], held.at[expert], load_sem.at[index, expert])

    for index in range(3):
        load(index, 0).start()

    barrier = pltpu.get_barrier_semaphore()

    @pl.when(has_left)
    def _():
        pl.semaphore_signal(barrier, inc=1, device_id={"et": p - 1}, device_id_type=MESH)

    @pl.when(has_right)
    def _():
        pl.semaphore_signal(barrier, inc=1, device_id={"et": p + 1}, device_id_type=MESH)

    plain, scaled = routing(ids[...], logits[...])
    weighted[...] = scaled
    for part in range(d_steps):
        columns = pl.ds(part * D_TILE, D_TILE)
        picked = jnp.dot(plain, tokens[:, columns], preferred_element_type=jnp.float32).astype(jnp.bfloat16)
        for c in range(count):
            rows[c, p, :, columns] = picked[c * ROWS : (c + 1) * ROWS]

    pl.semaphore_wait(barrier, jnp.where(has_left & has_right, 2, 1))

    def span(u):
        return pl.ds(pl.multiple_of(u * UNIT, UNIT), UNIT)

    def ag_copy(c, u, k, way, arriving=False):
        source = p - k if way == 0 else p + k
        held = rows.at[c, source, span(u)]
        step = k - 1 if arriving else k
        return pltpu.make_async_remote_copy(
            src_ref=held,
            dst_ref=held,
            send_sem=ag_send.at[way, c, u, step],
            recv_sem=ag_recv.at[way, c, u, step + 1],
            device_id={"et": p + 1 if (way == 0) != arriving else p - 1},
            device_id_type=MESH,
        )

    def ag_each(c, u, k, act):
        @pl.when((p - k >= 0) & has_right & (k < n - 1))
        def _():
            act(ag_copy(c, u, k, 0))

        @pl.when((p + k <= n - 1) & has_left & (k < n - 1))
        def _():
            act(ag_copy(c, u, k, 1))

    def ag_event(c, event):
        k, u = 1 + event // parts, event % parts

        @pl.when(p - k >= 0)
        def _():
            ag_copy(c, u, k, 0, True).wait_recv()

        @pl.when(p + k <= n - 1)
        def _():
            ag_copy(c, u, k, 1, True).wait_recv()

        ag_each(c, u, k, lambda copy: copy.start())

        @pl.when((k == n - 1) & (c + 1 < count))
        def _():
            ag_each(c + 1, u, 0, lambda copy: copy.start())

    def rs_copy(c, u, k, way, arriving=False):
        held = (right, left)[way]
        step = k + 1 if arriving else k
        return pltpu.make_async_remote_copy(
            src_ref=held.at[c, step, span(u)],
            dst_ref=held.at[c, step - 1, span(u)],
            send_sem=rs_send.at[way, c, u, step],
            recv_sem=rs_recv.at[way, c, u, step - 1],
            device_id={"et": p + 1 if (way == 0) != arriving else p - 1},
            device_id_type=MESH,
        )

    def rs_event(c, event):
        k, u = n - 1 - event // parts, event % parts
        for way in range(2):
            held = (right, left)[way]
            target = p + k if way == 0 else p - k
            exists = target <= n - 1 if way == 0 else target >= 0
            behind = has_left if way == 0 else has_right

            @pl.when(exists & behind)
            def _():
                rs_copy(c, u, k, way, True).wait_recv()
                summed = held[c, k, span(u)].astype(jnp.float32) + terms[c, target, span(u)].astype(jnp.float32)
                held[c, k, span(u)] = summed.astype(jnp.bfloat16)

            @pl.when(exists & jnp.logical_not(behind))
            def _():
                held[c, k, span(u)] = terms[c, target, span(u)]

            @pl.when(exists)
            def _():
                rs_copy(c, u, k, way).start()

    ag_events = (n - 1) * parts
    ag_inside = min(ag_events, AG_INSIDE * ag_events // 9)
    rs_events = (n - 2) * parts

    @pl.loop(0, parts)
    def _(u):
        ag_each(0, u, 0, lambda copy: copy.start())

    @pl.loop(0, ag_events)
    def _(event):
        ag_event(0, event)

    @pl.loop(0, count)
    def _(c):
        expert = c // per_expert
        first_use = c % per_expert == 0

        @pl.loop(0, steps)
        def _(i):
            @pl.when((i == 0) & first_use)
            def _():
                load(0, expert).wait()
                load(1, expert).wait()

            @pl.when((i == 0) & (c == 0))
            def _():
                for index in range(3):
                    load(index, 1).start()

            @pl.when((i == f_steps) & first_use)
            def _():
                load(2, expert).wait()

            @pl.when(i < f_steps)
            def _():
                at = pl.ds(pl.multiple_of(i * f_tile, f_tile) if f_steps > 1 else 0, f_tile)
                x = rows[c].reshape(m, features)
                dims = (((1,), (1,)), ((), ()))
                g = lax.dot_general(x, gate[expert, at, :], dims, preferred_element_type=jnp.float32)
                u = lax.dot_general(x, up[expert, at, :], dims, preferred_element_type=jnp.float32)
                hidden[:, at] = (g / (1.0 + jnp.exp(-g)) * u).astype(jnp.bfloat16)

            @pl.when(i >= f_steps)
            def _():
                at = pl.ds(pl.multiple_of((i - f_steps) * D_TILE, D_TILE), D_TILE)
                y = jnp.dot(hidden[...], down[expert, :, at], preferred_element_type=jnp.float32)
                terms[c, :, :, at] = y.astype(jnp.bfloat16).reshape(n, ROWS, D_TILE)

            @pl.when(c > 0)
            def _():
                @pl.loop(i * rs_events // steps, (i + 1) * rs_events // steps)
                def _(event):
                    rs_event(c - 1, parts + event)

            @pl.when(c + 1 < count)
            def _():
                @pl.loop(i * ag_inside // steps, (i + 1) * ag_inside // steps)
                def _(event):
                    ag_event(c + 1, event)

        @pl.loop(0, parts)
        def _(event):
            rs_event(c, event)

        @pl.when(c + 1 < count)
        def _():
            @pl.loop(ag_inside, ag_events)
            def _(event):
                ag_event(c + 1, event)

    @pl.loop(parts, parts + rs_events)
    def _(event):
        rs_event(count - 1, event)

    @pl.loop(0, count * parts)
    def _(unit):
        c, u = unit // parts, unit % parts
        total[...] = terms[c, p, span(u)].astype(jnp.float32)

        @pl.when(has_left)
        def _():
            rs_copy(c, u, 0, 0, True).wait_recv()
            total[...] += right[c, 0, span(u)].astype(jnp.float32)

        @pl.when(has_right)
        def _():
            rs_copy(c, u, 0, 1, True).wait_recv()
            total[...] += left[c, 0, span(u)].astype(jnp.float32)

        own[span(unit), :] = total[...].astype(jnp.bfloat16)

    @pl.loop(0, count * parts)
    def _(unit):
        c, u = unit // parts, unit % parts

        @pl.loop(0, n - 1)
        def _(k):
            ag_each(c, u, k, lambda copy: copy.wait_send())

            @pl.when(p + k + 1 <= n - 1)
            def _():
                rs_copy(c, u, k + 1, 0).wait_send()

            @pl.when(p - k - 1 >= 0)
            def _():
                rs_copy(c, u, k + 1, 1).wait_send()


def body(n, tokens, expert_ids, route_logits, w_gate, w_up, w_down):
    count, features, units = EXP_WIN * CAP // ROWS, tokens.shape[1], w_gate.shape[1]
    blocks = pltpu.VMEM((count, n, ROWS, features), jnp.bfloat16)
    semaphores = pltpu.SemaphoreType.DMA((2, count, ROWS // UNIT, n))
    vmem = pl.BlockSpec(memory_space=pltpu.VMEM)
    hbm = pl.BlockSpec(memory_space=pl.ANY)
    weights = pltpu.VMEM((EXP_WIN, units, features), jnp.bfloat16)
    own, weighted = pl.pallas_call(
        functools.partial(kernel, n),
        out_shape=(
            jax.ShapeDtypeStruct((EXP_WIN * CAP, features), jnp.bfloat16),
            jax.ShapeDtypeStruct((EXP_WIN * CAP, tokens.shape[0]), jnp.bfloat16),
        ),
        in_specs=[vmem, vmem, vmem, hbm, hbm, hbm],
        out_specs=(vmem, vmem),
        scratch_shapes=[
            blocks,
            blocks,
            blocks,
            blocks,
            weights,
            weights,
            weights,
            pltpu.VMEM((n * ROWS, units), jnp.bfloat16),
            pltpu.VMEM((UNIT, features), jnp.float32),
            pltpu.SemaphoreType.DMA((3, EXP_WIN)),
            semaphores,
            semaphores,
            semaphores,
            semaphores,
        ],
        compiler_params=pltpu.CompilerParams(collective_id=0, has_side_effects=True, vmem_limit_bytes=60 * 2**20),
    )(tokens, expert_ids.T, route_logits.T, w_gate, w_up, w_down)
    mixed = lax.dot_general(weighted, own, (((0,), (0,)), ((), ())), preferred_element_type=jnp.float32)
    return mixed.astype(jnp.bfloat16)


def solution(mesh):
    in_specs = (
        P(("rep", "et"), None),
        P(("rep", "et"), None),
        P(("rep", "et"), None),
        P(None, "et", None),
        P(None, "et", None),
        P(None, "et", None),
    )
    out_specs = P(("rep", "et"), None)
    return jax.shard_map(
        functools.partial(body, mesh.shape["et"]), mesh=mesh, in_specs=in_specs, out_specs=out_specs, check_vma=False
    )
```

time: 125 us -> 62.7 us (0.50)
  waiting for transfers between devices: 61.5 us -> 0 us
  Pallas kernels: 0 us -> 60.4 us
  matrix products: 33.8 us -> 2.13 us
  between operations: 13.4 us -> 0.01 us
  blocking collectives: 12.5 us -> 0 us
  other arithmetic: 3.03 us -> 0 us
    pallas_call x0 -> x1, Pallas kernels: none -> 60.4 us  [body(): pl.pallas_call(functools.partial(kernel, n), out_shape=(jax.ShapeDtypeStr...]
    reduce_scatter x1 -> x0, waiting for transfers between devices: 34.3 us -> none  [body(): lax.psum_scatter(partial_value, 'et', scatter_dimension=1, tiled=True)]
    dot_general x6 -> x1, matrix products: 33.8 us -> 2.13 us  [body(): lax.dot_general(weighted, own, (((0,), (0,)), ((), ())), preferred_elemen...]
    all_gather x1 -> x0, waiting for transfers between devices: 27.1 us -> none  [body(): lax.all_gather(token_rows, 'et', axis=1, tiled=True)]
    all_gather x1 -> x0, blocking collectives: 12.5 us -> none  [body(): lax.all_gather(weights, 'et', axis=1, tiled=True)]
    reduce_sum x2 -> x0, other arithmetic: 1.39 us -> none  [the longest x1 0.7 us: body(): jnp.sum(jnp.where(chosen, probs_wide[:, :, None], jnp.float32(0.0)), axis=1)]
  transfers between devices with their start and end apart: 2 -> 0, of which waited for: 2 -> 0; matrix products, arithmetic and copies ran while one was open for 0% -> 0% of each run, Pallas kernels for 0% -> 0%
where the time goes in v5:
time: 62.7 us; the launch traced here: 62.5 us
  Pallas kernels  60.4 us (96%)
  matrix products  2.13 us (3%)
    pallas_call x1, Pallas kernels, body(): pl.pallas_call(functools.partial(kernel, n), out_shape=(jax.ShapeDtypeStr...  60.4 us
    dot_general x1, matrix products, body(): lax.dot_general(weighted, own, (((0,), (0,)), ((), ())), preferred_elemen...  2.13 us

profile of v5, /device:TPU:0, one launch (start us, length us, event | category | flops | bytes accessed | tf_op | source)
XLA Modules:
  0.0 62.5 jit_solution(5994008438510243975)
XLA Ops:
  0.0 60.4 %shard_map.64 = (bf16[96,2048]{1,0:T(8,128)(2,1)}, bf16[96,128]{1,0:T(8,128)(2,1)}) custom-call(bf16[128,2048]{1,0:T(8,128)(2,1)} %tokens.1, s32[2,128]{1,0:T(2,128)} %bitcast.4, f32[2,128]{1,0:T(2,128)} %bitcast.5, bf16[2,1792,2048]{2,1,0:T(8,128)(2,1)} %w_gate.1, bf16[2,1792,2048]{2,1,0:T(8,128)(2,1)} %w_up.1, bf16[2,1792,2048]{2,1,0:T(8,128)(2,1)} %w_down.1), custom_call_target="tpu_custom_call" | custom-call | tf_op jit(solution)/shard_map/pallas_call | solution.py:272
  60.4 2.1 %convolution_convert_fusion = bf16[128,2048]{1,0:T(8,128)(2,1)} fusion(bf16[96,128]{1,0:T(8,128)(2,1)} %get-tuple-element.7, bf16[96,2048]{1,0:T(8,128)(2,1)} %get-tuple-element.8), kind=kOutput, calls=%fused_computation | convolution fusion | flops 50593792 | bytes 942080 | tf_op jit(solution)/shard_map/dot_general | solution.py:298

commit v6 on v5

--- a/solution.py
+++ b/solution.py
@@ -11,7 +11,7 @@
 CAP = 48
 ROWS = 48
 UNIT = 16
-F_TILE = 256
+F_TILE = 896
 D_TILE = 512
 AG_INSIDE = 5
 MESH = pl.DeviceIdType.MESH
@@ -40,7 +40,7 @@
 
 
 def kernel(n, tokens, ids, logits, w_gate, w_up, w_down, own, weighted, *scratch):
-    rows, terms, right, left, gate, up, down, hidden, total, load_sem, ag_send, ag_recv, rs_send, rs_recv = scratch
+    rows, terms, right, left, gate, up, down, turned, hidden, total, load_sem, ag_send, ag_recv, rs_send, rs_recv = scratch
     p = lax.axis_index("et")
     features, units = tokens.shape[1], gate.shape[1]
     count, parts = EXP_WIN * CAP // ROWS, ROWS // UNIT
@@ -171,6 +171,11 @@
         expert = c // per_expert
         first_use = c % per_expert == 0
 
+        @pl.loop(0, d_steps)
+        def _(j):
+            at = pl.ds(pl.multiple_of(j * D_TILE, D_TILE), D_TILE)
+            turned[at, :] = rows[c, :, :, at].reshape(m, D_TILE).T
+
         @pl.loop(0, steps)
         def _(i):
             @pl.when((i == 0) & first_use)
@@ -190,11 +195,9 @@
             @pl.when(i < f_steps)
             def _():
                 at = pl.ds(pl.multiple_of(i * f_tile, f_tile) if f_steps > 1 else 0, f_tile)
-                x = rows[c].reshape(m, features)
-                dims = (((1,), (1,)), ((), ()))
-                g = lax.dot_general(x, gate[expert, at, :], dims, preferred_element_type=jnp.float32)
-                u = lax.dot_general(x, up[expert, at, :], dims, preferred_element_type=jnp.float32)
-                hidden[:, at] = (g / (1.0 + jnp.exp(-g)) * u).astype(jnp.bfloat16)
+                g = jnp.dot(gate[expert, at, :], turned[...], preferred_element_type=jnp.float32)
+                u = jnp.dot(up[expert, at, :], turned[...], preferred_element_type=jnp.float32)
+                hidden[:, at] = (g / (1.0 + jnp.exp(-g)) * u).astype(jnp.bfloat16).T
 
             @pl.when(i >= f_steps)
             def _():
@@ -285,6 +288,7 @@
             weights,
             weights,
             weights,
+            pltpu.VMEM((features, n * ROWS), jnp.bfloat16),
             pltpu.VMEM((n * ROWS, units), jnp.bfloat16),
             pltpu.VMEM((UNIT, features), jnp.float32),
             pltpu.SemaphoreType.DMA((3, EXP_WIN)),

time: 62.7 us -> 62.9 us (level)
  no operation moved by 1% of the time
where the time goes in v6:
time: 62.9 us; the launch traced here: 62.8 us
  Pallas kernels  60.6 us (96%)
  matrix products  2.13 us (3%)
    pallas_call x1, Pallas kernels, body(): pl.pallas_call(functools.partial(kernel, n), out_shape=(jax.ShapeDtypeStr...  60.6 us
    dot_general x1, matrix products, body(): lax.dot_general(weighted, own, (((0,), (0,)), ((), ())), preferred_elemen...  2.13 us

profile of v6, /device:TPU:0, one launch (start us, length us, event | category | flops | bytes accessed | tf_op | source)
XLA Modules:
  0.0 62.8 jit_solution(8948285415740064940)
XLA Ops:
  0.0 60.6 %shard_map.64 = (bf16[96,2048]{1,0:T(8,128)(2,1)}, bf16[96,128]{1,0:T(8,128)(2,1)}) custom-call(bf16[128,2048]{1,0:T(8,128)(2,1)} %tokens.1, s32[2,128]{1,0:T(2,128)} %bitcast.4, f32[2,128]{1,0:T(2,128)} %bitcast.5, bf16[2,1792,2048]{2,1,0:T(8,128)(2,1)} %w_gate.1, bf16[2,1792,2048]{2,1,0:T(8,128)(2,1)} %w_up.1, bf16[2,1792,2048]{2,1,0:T(8,128)(2,1)} %w_down.1), custom_call_target="tpu_custom_call" | custom-call | tf_op jit(solution)/shard_map/pallas_call | solution.py:275
  60.6 2.1 %convolution_convert_fusion = bf16[128,2048]{1,0:T(8,128)(2,1)} fusion(bf16[96,128]{1,0:T(8,128)(2,1)} %get-tuple-element.7, bf16[96,2048]{1,0:T(8,128)(2,1)} %get-tuple-element.8), kind=kOutput, calls=%fused_computation | convolution fusion | flops 50593792 | bytes 942080 | tf_op jit(solution)/shard_map/dot_general | solution.py:302

commit v7 on v5

--- a/solution.py
+++ b/solution.py
@@ -9,11 +9,11 @@
 
 EXP_WIN = 2
 CAP = 48
-ROWS = 48
+ROWS = 16
 UNIT = 16
 F_TILE = 256
 D_TILE = 512
-AG_INSIDE = 5
+AG_INSIDE = 6
 MESH = pl.DeviceIdType.MESH
 
 
@@ -116,7 +116,7 @@
 
         ag_each(c, u, k, lambda copy: copy.start())
 
-        @pl.when((k == n - 1) & (c + 1 < count))
+        @pl.when((k == 1) & (c + 1 < count))
         def _():
             ag_each(c + 1, u, 0, lambda copy: copy.start())
 
@@ -162,6 +162,9 @@
     def _(u):
         ag_each(0, u, 0, lambda copy: copy.start())
 
+    for index in range(3):
+        load(index, 1).start()
+
     @pl.loop(0, ag_events)
     def _(event):
         ag_event(0, event)
@@ -177,11 +180,6 @@
             def _():
                 load(0, expert).wait()
                 load(1, expert).wait()
-
-            @pl.when((i == 0) & (c == 0))
-            def _():
-                for index in range(3):
-                    load(index, 1).start()
 
             @pl.when((i == f_steps) & first_use)
             def _():

time: 62.7 us -> 95.5 us (1.52)
  Pallas kernels: 60.4 us -> 92.6 us
    pallas_call x1, Pallas kernels: 60.4 us -> 92.6 us  [body(): pl.pallas_call(functools.partial(kernel, n), out_shape=(jax.ShapeDtypeStr...]
where the time goes in v7:
time: 95.5 us; the launch traced here: 94.7 us
  Pallas kernels  92.6 us (97%)
  matrix products  2.13 us (2%)
    pallas_call x1, Pallas kernels, body(): pl.pallas_call(functools.partial(kernel, n), out_shape=(jax.ShapeDtypeStr...  92.6 us
    dot_general x1, matrix products, body(): lax.dot_general(weighted, own, (((0,), (0,)), ((), ())), preferred_elemen...  2.13 us

profile of v7, /device:TPU:0, one launch (start us, length us, event | category | flops | bytes accessed | tf_op | source)
XLA Modules:
  0.0 94.7 jit_solution(1685713945112919345)
XLA Ops:
  0.0 92.6 %shard_map.64 = (bf16[96,2048]{1,0:T(8,128)(2,1)}, bf16[96,128]{1,0:T(8,128)(2,1)}) custom-call(bf16[128,2048]{1,0:T(8,128)(2,1)} %tokens.1, s32[2,128]{1,0:T(2,128)} %bitcast.4, f32[2,128]{1,0:T(2,128)} %bitcast.5, bf16[2,1792,2048]{2,1,0:T(8,128)(2,1)} %w_gate.1, bf16[2,1792,2048]{2,1,0:T(8,128)(2,1)} %w_up.1, bf16[2,1792,2048]{2,1,0:T(8,128)(2,1)} %w_down.1), custom_call_target="tpu_custom_call" | custom-call | tf_op jit(solution)/shard_map/pallas_call | solution.py:270
  92.6 2.1 %convolution_convert_fusion = bf16[128,2048]{1,0:T(8,128)(2,1)} fusion(bf16[96,128]{1,0:T(8,128)(2,1)} %get-tuple-element.7, bf16[96,2048]{1,0:T(8,128)(2,1)} %get-tuple-element.8), kind=kOutput, calls=%fused_computation | convolution fusion | flops 50593792 | bytes 942080 | tf_op jit(solution)/shard_map/dot_general | solution.py:296

commit v8 on v7

--- a/solution.py
+++ b/solution.py
@@ -9,11 +9,11 @@
 
 EXP_WIN = 2
 CAP = 48
-ROWS = 16
+ROWS = 48
 UNIT = 16
 F_TILE = 256
 D_TILE = 512
-AG_INSIDE = 6
+AG_INSIDE = 5
 MESH = pl.DeviceIdType.MESH
 
 
@@ -116,16 +116,19 @@
 
         ag_each(c, u, k, lambda copy: copy.start())
 
-        @pl.when((k == 1) & (c + 1 < count))
+        @pl.when((k == n - 1) & (c + 1 < count))
         def _():
             ag_each(c + 1, u, 0, lambda copy: copy.start())
+
+    def band(u):
+        return pl.ds(pl.multiple_of(u * D_TILE, D_TILE), D_TILE)
 
     def rs_copy(c, u, k, way, arriving=False):
         held = (right, left)[way]
         step = k + 1 if arriving else k
         return pltpu.make_async_remote_copy(
-            src_ref=held.at[c, step, span(u)],
-            dst_ref=held.at[c, step - 1, span(u)],
+            src_ref=held.at[c, step, :, band(u)],
+            dst_ref=held.at[c, step - 1, :, band(u)],
             send_sem=rs_send.at[way, c, u, step],
             recv_sem=rs_recv.at[way, c, u, step - 1],
             device_id={"et": p + 1 if (way == 0) != arriving else p - 1},
@@ -133,7 +136,7 @@
         )
 
     def rs_event(c, event):
-        k, u = n - 1 - event // parts, event % parts
+        k, u = n - 1 - event // d_steps, event % d_steps
         for way in range(2):
             held = (right, left)[way]
             target = p + k if way == 0 else p - k
@@ -143,12 +146,12 @@
             @pl.when(exists & behind)
             def _():
                 rs_copy(c, u, k, way, True).wait_recv()
-                summed = held[c, k, span(u)].astype(jnp.float32) + terms[c, target, span(u)].astype(jnp.float32)
-                held[c, k, span(u)] = summed.astype(jnp.bfloat16)
+                summed = held[c, k, :, band(u)].astype(jnp.float32) + terms[c, target, :, band(u)].astype(jnp.float32)
+                held[c, k, :, band(u)] = summed.astype(jnp.bfloat16)
 
             @pl.when(exists & jnp.logical_not(behind))
             def _():
-                held[c, k, span(u)] = terms[c, target, span(u)]
+                held[c, k, :, band(u)] = terms[c, target, :, band(u)]
 
             @pl.when(exists)
             def _():
@@ -156,7 +159,7 @@
 
     ag_events = (n - 1) * parts
     ag_inside = min(ag_events, AG_INSIDE * ag_events // 9)
-    rs_events = (n - 2) * parts
+    rs_events = (n - 2) * d_steps
 
     @pl.loop(0, parts)
     def _(u):
@@ -199,12 +202,13 @@
                 at = pl.ds(pl.multiple_of((i - f_steps) * D_TILE, D_TILE), D_TILE)
                 y = jnp.dot(hidden[...], down[expert, :, at], preferred_element_type=jnp.float32)
                 terms[c, :, :, at] = y.astype(jnp.bfloat16).reshape(n, ROWS, D_TILE)
+                rs_event(c, i - f_steps)
 
             @pl.when(c > 0)
             def _():
                 @pl.loop(i * rs_events // steps, (i + 1) * rs_events // steps)
                 def _(event):
-                    rs_event(c - 1, parts + event)
+                    rs_event(c - 1, d_steps + event)
 
             @pl.when(c + 1 < count)
             def _():
@@ -212,44 +216,42 @@
                 def _(event):
                     ag_event(c + 1, event)
 
-        @pl.loop(0, parts)
-        def _(event):
-            rs_event(c, event)
-
         @pl.when(c + 1 < count)
         def _():
             @pl.loop(ag_inside, ag_events)
             def _(event):
                 ag_event(c + 1, event)
 
-    @pl.loop(parts, parts + rs_events)
+    @pl.loop(d_steps, d_steps + rs_events)
     def _(event):
         rs_event(count - 1, event)
 
-    @pl.loop(0, count * parts)
+    @pl.loop(0, count * d_steps)
     def _(unit):
-        c, u = unit // parts, unit % parts
-        total[...] = terms[c, p, span(u)].astype(jnp.float32)
+        c, u = unit // d_steps, unit % d_steps
+        total[...] = terms[c, p, :, band(u)].astype(jnp.float32)
 
         @pl.when(has_left)
         def _():
             rs_copy(c, u, 0, 0, True).wait_recv()
-            total[...] += right[c, 0, span(u)].astype(jnp.float32)
+            total[...] += right[c, 0, :, band(u)].astype(jnp.float32)
 
         @pl.when(has_right)
         def _():
             rs_copy(c, u, 0, 1, True).wait_recv()
-            total[...] += left[c, 0, span(u)].astype(jnp.float32)
-
-        own[span(unit), :] = total[...].astype(jnp.bfloat16)
-
-    @pl.loop(0, count * parts)
-    def _(unit):
-        c, u = unit // parts, unit % parts
-
-        @pl.loop(0, n - 1)
-        def _(k):
-            ag_each(c, u, k, lambda copy: copy.wait_send())
+            total[...] += left[c, 0, :, band(u)].astype(jnp.float32)
+
+        own[pl.ds(pl.multiple_of(c * ROWS, ROWS), ROWS), band(u)] = total[...].astype(jnp.bfloat16)
+
+    @pl.loop(0, n - 1)
+    def _(k):
+        @pl.loop(0, count * parts)
+        def _(unit):
+            ag_each(unit // parts, unit % parts, k, lambda copy: copy.wait_send())
+
+        @pl.loop(0, count * d_steps)
+        def _(unit):
+            c, u = unit // d_steps, unit % d_steps
 
             @pl.when(p + k + 1 <= n - 1)
             def _():
@@ -263,7 +265,8 @@
 def body(n, tokens, expert_ids, route_logits, w_gate, w_up, w_down):
     count, features, units = EXP_WIN * CAP // ROWS, tokens.shape[1], w_gate.shape[1]
     blocks = pltpu.VMEM((count, n, ROWS, features), jnp.bfloat16)
-    semaphores = pltpu.SemaphoreType.DMA((2, count, ROWS // UNIT, n))
+    gather_semaphores = pltpu.SemaphoreType.DMA((2, count, ROWS // UNIT, n))
+    sum_semaphores = pltpu.SemaphoreType.DMA((2, count, features // D_TILE, n))
     vmem = pl.BlockSpec(memory_space=pltpu.VMEM)
     hbm = pl.BlockSpec(memory_space=pl.ANY)
     weights = pltpu.VMEM((EXP_WIN, units, features), jnp.bfloat16)
@@ -284,12 +287,12 @@
             weights,
             weights,
             pltpu.VMEM((n * ROWS, units), jnp.bfloat16),
-            pltpu.VMEM((UNIT, features), jnp.float32),
+            pltpu.VMEM((ROWS, D_TILE), jnp.float32),
             pltpu.SemaphoreType.DMA((3, EXP_WIN)),
-            semaphores,
-            semaphores,
-            semaphores,
-            semaphores,
+            gather_semaphores,
+            gather_semaphores,
+            sum_semaphores,
+            sum_semaphores,
         ],
         compiler_params=pltpu.CompilerParams(collective_id=0, has_side_effects=True, vmem_limit_bytes=60 * 2**20),
     )(tokens, expert_ids.T, route_logits.T, w_gate, w_up, w_down)

time: 95.5 us -> 62.7 us (0.66)
  Pallas kernels: 92.6 us -> 60.4 us
    pallas_call x1, Pallas kernels: 92.6 us -> 60.4 us  [body(): pl.pallas_call(functools.partial(kernel, n), out_shape=(jax.ShapeDtypeStr...]
where the time goes in v8:
time: 62.7 us; the launch traced here: 62.5 us
  Pallas kernels  60.4 us (96%)
  matrix products  2.13 us (3%)
    pallas_call x1, Pallas kernels, body(): pl.pallas_call(functools.partial(kernel, n), out_shape=(jax.ShapeDtypeStr...  60.4 us
    dot_general x1, matrix products, body(): lax.dot_general(weighted, own, (((0,), (0,)), ((), ())), preferred_elemen...  2.13 us

profile of v8, /device:TPU:0, one launch (start us, length us, event | category | flops | bytes accessed | tf_op | source)
XLA Modules:
  0.0 62.5 jit_solution(9745629959520402900)
XLA Ops:
  0.0 60.4 %shard_map.64 = (bf16[96,2048]{1,0:T(8,128)(2,1)}, bf16[96,128]{1,0:T(8,128)(2,1)}) custom-call(bf16[128,2048]{1,0:T(8,128)(2,1)} %tokens.1, s32[2,128]{1,0:T(2,128)} %bitcast.4, f32[2,128]{1,0:T(2,128)} %bitcast.5, bf16[2,1792,2048]{2,1,0:T(8,128)(2,1)} %w_gate.1, bf16[2,1792,2048]{2,1,0:T(8,128)(2,1)} %w_up.1, bf16[2,1792,2048]{2,1,0:T(8,128)(2,1)} %w_down.1), custom_call_target="tpu_custom_call" | custom-call | tf_op jit(solution)/shard_map/pallas_call | solution.py:273
  60.4 2.1 %convolution_convert_fusion = bf16[128,2048]{1,0:T(8,128)(2,1)} fusion(bf16[96,128]{1,0:T(8,128)(2,1)} %get-tuple-element.7, bf16[96,2048]{1,0:T(8,128)(2,1)} %get-tuple-element.8), kind=kOutput, calls=%fused_computation | convolution fusion | flops 50593792 | bytes 942080 | tf_op jit(solution)/shard_map/dot_general | solution.py:299

commit v9 on v8

--- a/solution.py
+++ b/solution.py
@@ -13,7 +13,7 @@
 UNIT = 16
 F_TILE = 256
 D_TILE = 512
-AG_INSIDE = 5
+AG_INSIDE = 9
 MESH = pl.DeviceIdType.MESH
 
 
@@ -116,7 +116,7 @@
 
         ag_each(c, u, k, lambda copy: copy.start())
 
-        @pl.when((k == n - 1) & (c + 1 < count))
+        @pl.when((k == max(n - 2, 1)) & (c + 1 < count))
         def _():
             ag_each(c + 1, u, 0, lambda copy: copy.start())
 

time: 62.7 us -> 63.5 us (1.013)
  Pallas kernels: 60.4 us -> 61.2 us
    pallas_call x1, Pallas kernels: 60.4 us -> 61.2 us  [body(): pl.pallas_call(functools.partial(kernel, n), out_shape=(jax.ShapeDtypeStr...]
where the time goes in v9:
time: 63.5 us; the launch traced here: 63.3 us
  Pallas kernels  61.2 us (96%)
  matrix products  2.14 us (3%)
    pallas_call x1, Pallas kernels, body(): pl.pallas_call(functools.partial(kernel, n), out_shape=(jax.ShapeDtypeStr...  61.2 us
    dot_general x1, matrix products, body(): lax.dot_general(weighted, own, (((0,), (0,)), ((), ())), preferred_elemen...  2.14 us

profile of v9, /device:TPU:0, one launch (start us, length us, event | category | flops | bytes accessed | tf_op | source)
XLA Modules:
  0.0 63.3 jit_solution(9824994242987087654)
XLA Ops:
  0.0 61.2 %shard_map.64 = (bf16[96,2048]{1,0:T(8,128)(2,1)}, bf16[96,128]{1,0:T(8,128)(2,1)}) custom-call(bf16[128,2048]{1,0:T(8,128)(2,1)} %tokens.1, s32[2,128]{1,0:T(2,128)} %bitcast.4, f32[2,128]{1,0:T(2,128)} %bitcast.5, bf16[2,1792,2048]{2,1,0:T(8,128)(2,1)} %w_gate.1, bf16[2,1792,2048]{2,1,0:T(8,128)(2,1)} %w_up.1, bf16[2,1792,2048]{2,1,0:T(8,128)(2,1)} %w_down.1), custom_call_target="tpu_custom_call" | custom-call | tf_op jit(solution)/shard_map/pallas_call | solution.py:273
  61.2 2.1 %convolution_convert_fusion = bf16[128,2048]{1,0:T(8,128)(2,1)} fusion(bf16[96,128]{1,0:T(8,128)(2,1)} %get-tuple-element.7, bf16[96,2048]{1,0:T(8,128)(2,1)} %get-tuple-element.8), kind=kOutput, calls=%fused_computation | convolution fusion | flops 50593792 | bytes 942080 | tf_op jit(solution)/shard_map/dot_general | solution.py:299

commit v10 on v9

--- a/solution.py
+++ b/solution.py
@@ -13,7 +13,7 @@
 UNIT = 16
 F_TILE = 256
 D_TILE = 512
-AG_INSIDE = 9
+AG_INSIDE = 5
 MESH = pl.DeviceIdType.MESH
 
 

time: 63.5 us -> 63.5 us (level)
  no operation moved by 1% of the time
where the time goes in v10:
time: 63.5 us; the launch traced here: 63.3 us
  Pallas kernels  61.2 us (96%)
  matrix products  2.13 us (3%)
    pallas_call x1, Pallas kernels, body(): pl.pallas_call(functools.partial(kernel, n), out_shape=(jax.ShapeDtypeStr...  61.2 us
    dot_general x1, matrix products, body(): lax.dot_general(weighted, own, (((0,), (0,)), ((), ())), preferred_elemen...  2.13 us

profile of v10, /device:TPU:0, one launch (start us, length us, event | category | flops | bytes accessed | tf_op | source)
XLA Modules:
  0.0 63.3 jit_solution(14111903372204826826)
XLA Ops:
  0.0 61.2 %shard_map.64 = (bf16[96,2048]{1,0:T(8,128)(2,1)}, bf16[96,128]{1,0:T(8,128)(2,1)}) custom-call(bf16[128,2048]{1,0:T(8,128)(2,1)} %tokens.1, s32[2,128]{1,0:T(2,128)} %bitcast.4, f32[2,128]{1,0:T(2,128)} %bitcast.5, bf16[2,1792,2048]{2,1,0:T(8,128)(2,1)} %w_gate.1, bf16[2,1792,2048]{2,1,0:T(8,128)(2,1)} %w_up.1, bf16[2,1792,2048]{2,1,0:T(8,128)(2,1)} %w_down.1), custom_call_target="tpu_custom_call" | custom-call | tf_op jit(solution)/shard_map/pallas_call | solution.py:273
  61.2 2.1 %convolution_convert_fusion = bf16[128,2048]{1,0:T(8,128)(2,1)} fusion(bf16[96,128]{1,0:T(8,128)(2,1)} %get-tuple-element.7, bf16[96,2048]{1,0:T(8,128)(2,1)} %get-tuple-element.8), kind=kOutput, calls=%fused_computation | convolution fusion | flops 50593792 | bytes 942080 | tf_op jit(solution)/shard_map/dot_general | solution.py:299
